TPU v7x, 512 devices: a whole 4x4x16 slice. The times are simulated.
512 devices in a mesh: freq: 8 (over y, core), tm: 64 (over z, x).
Axes of the slice: x: 4, y: 4, z: 16, core: 2. Of those that a mesh axis runs over, the one named last changes fastest.
Arguments:
- audio: bfloat16 [64, 8388608], P('tm', 'freq'), may hold values from -8 to 8
- w_start: float32 [32, 4096], P(None, 'freq'), may hold values from 0.05 to 0.5
- h_start: float32 [32, 65536], P(None, 'tm'), may hold values from 0.05 to 0.5
Outputs:
- components: float32 [32, 4096], P(None, 'freq')
- activations: float32 [32, 65536], P(None, 'tm')
All inputs are finite; a program needn't handle non-finite values.
Results may differ from a plain program's by a relative error of at most 0.00053.
Values may be sent and summed in bfloat16 or wider, within the bound.
A program may use at most 64 MiB of HBM per device.

v0:
```python
import math

import jax
import jax.numpy as jnp
from jax import lax
from jax.sharding import PartitionSpec as P

BINS = 4096
ITERS = 2


def spectrum_slab(audio, bins):
    frame_len = 2 * bins
    inner_len = 128
    outer_len = frame_len // inner_len
    highest = lax.Precision.HIGHEST
    samples = audio.reshape(-1, outer_len, inner_len).astype(jnp.float32)
    outer_idx = jnp.arange(outer_len)
    inner_idx = jnp.arange(inner_len)
    position = (outer_idx[:, None] * inner_len + inner_idx[None, :]).astype(jnp.float32)
    window = 0.5 - 0.5 * jnp.cos(2.0 * math.pi * position / frame_len)
    samples = samples * window
    first_angle = (
        2.0
        * math.pi
        * (outer_idx[:, None] * outer_idx[None, :] % outer_len).astype(jnp.float32)
        / outer_len
    )
    first_real = jnp.einsum("fan,ak->fkn", samples, jnp.cos(first_angle), precision=highest)
    first_imag = -jnp.einsum("fan,ak->fkn", samples, jnp.sin(first_angle), precision=highest)
    twist_angle = (
        2.0
        * math.pi
        * (outer_idx[:, None] * inner_idx[None, :] % frame_len).astype(jnp.float32)
        / frame_len
    )
    twist_cos = jnp.cos(twist_angle)
    twist_sin = jnp.sin(twist_angle)
    turned_real = first_real * twist_cos + first_imag * twist_sin
    turned_imag = first_imag * twist_cos - first_real * twist_sin
    half_idx = jnp.arange(inner_len // 2)
    second_angle = (
        2.0
        * math.pi
        * (inner_idx[:, None] * half_idx[None, :] % inner_len).astype(jnp.float32)
        / inner_len
    )
    second_cos = jnp.cos(second_angle)
    second_sin = jnp.sin(second_angle)
    bins_real = jnp.einsum("fkn,nb->fbk", turned_real, second_cos, precision=highest) + jnp.einsum(
        "fkn,nb->fbk", turned_imag, second_sin, precision=highest
    )
    bins_imag = jnp.einsum("fkn,nb->fbk", turned_imag, second_cos, precision=highest) - jnp.einsum(
        "fkn,nb->fbk", turned_real, second_sin, precision=highest
    )
    factor = 1.0 / math.sqrt(0.375 * frame_len)
    magnitude = jnp.sqrt(bins_real * bins_real + bins_imag * bins_imag) * factor
    return magnitude.reshape(magnitude.shape[0], -1).astype(jnp.bfloat16)


def refine(state, numer, gram):
    return state * numer / jnp.dot(gram, state, precision=lax.Precision.HIGHEST)


def shards(audio, w_start, h_start):
    highest = lax.Precision.HIGHEST
    magnitude = spectrum_slab(audio, BINS)
    grid = lax.all_to_all(magnitude, "freq", split_axis=1, concat_axis=0, tiled=True)
    components = w_start
    activations = h_start
    for step in range(ITERS):
        numer_h = jnp.einsum(
            "kb,fb->kf", components.astype(jnp.bfloat16), grid, preferred_element_type=jnp.float32
        )
        gram_w = jnp.dot(components, components.T, precision=highest)
        numer_h, gram_w = lax.psum((numer_h, gram_w), "freq")
        activations = refine(activations, numer_h, gram_w)
        numer_w = jnp.einsum(
            "kf,fb->kb", activations.astype(jnp.bfloat16), grid, preferred_element_type=jnp.float32
        )
        gram_h = jnp.dot(activations, activations.T, precision=highest)
        numer_w, gram_h = lax.psum((numer_w, gram_h), "tm")
        components = refine(components, numer_w, gram_h)
    return (components, activations)


def solution(mesh):
    placed = (P("tm", "freq"), P(None, "freq"), P(None, "tm"))
    return jax.shard_map(
        shards,
        mesh=mesh,
        in_specs=placed,
        out_specs=(P(None, "freq"), P(None, "tm")),
        check_vma=False,
    )
```

profile of v0, /device:TPU:8, one launch (start us, length us, event | category | flops | bytes accessed | tf_op | source)
XLA Modules:
  0.0 792.7 jit_solution(14402242608954847028)
XLA Ops:
  7.2 0.1 fusion.52
  7.4 7.0 convert_element_type.74
  14.4 0.2 multiply_subtract_fusion
  14.6 4.2 fusion.8
  18.8 5.3 add_bitcast_fusion
  24.1 6.9 fusion
  31.0 6.6 fusion.2
  37.5 6.7 fusion.4
  44.3 7.1 fusion.16
  51.4 0.7 copy.13
  52.1 22.9 %all_to_all.16 = bf16[128,8,512]{0,2,1:T(8,128)(2,1)S(1)} all-to-all(bf16[128,8,512]{0,2,1:T(8,128)(2,1)S(1)} %bitcast.56), channel_id=1, replica_groups=mesh['freq'=8,'tm'=64] {'freq'}, dimensions={1} | all-to-all | bytes 2097152 | tf_op jit(solution)/shard_map/all_to_all | solution.py:68
  75.0 0.5 copy.14
  75.6 1.1 convolution_bitcast_fusion
  76.7 0.0 all-reduce.7.cloned.1.call-start
  76.7 0.2 fusion.90
  76.9 21.6 %psum.57 = f32[32,32]{1,0:T(8,128)S(1)} all-reduce(f32[32,32]{1,0:T(8,128)S(1)} %fusion.90), channel_id=1, replica_groups=mesh['freq'=8,'tm'=64] {'freq'}, use_global_device_ids=true, to_apply=%region_1.2 | all-reduce | flops 1024 | bytes 8192 | tf_op jit(solution)/shard_map/psum | solution.py:76
  98.5 50.7 %all-reduce.5.cloned.1.call-done = f32[32,1024]{1,0:T(8,128)} async-done(((f32[32,1024]{1,0:T(8,128)}), f32[32,1024]{1,0:T(8,128)}) %all-reduce.5.cloned.1.call-update) | async-done | bytes 131088 | tf_op jit(solution)/shard_map/psum | solution.py:76
  149.2 1.2 convolution_divide_fusion.1
  150.4 0.9 fusion.21
  151.4 0.2 fusion.91
  151.6 280.1 %psum.59 = f32[32,32]{1,0:T(8,128)S(1)} all-reduce(f32[32,32]{1,0:T(8,128)S(1)} %fusion.91), channel_id=1, replica_groups=mesh['freq'=8,'tm'=64] {'tm'}, use_global_device_ids=true, to_apply=%region_3.4 | all-reduce | flops 1024 | bytes 8192 | tf_op jit(solution)/shard_map/psum | solution.py:82
  431.8 1.0 convolution_divide_fusion.3
  432.8 1.1 fusion.38
  433.9 0.0 all-reduce.11.cloned.1.call-start
  434.0 0.2 fusion.92
  434.2 22.8 %psum.61 = f32[32,32]{1,0:T(8,128)S(1)} all-reduce(f32[32,32]{1,0:T(8,128)S(1)} %fusion.92), channel_id=1, replica_groups=mesh['freq'=8,'tm'=64] {'freq'}, use_global_device_ids=true, to_apply=%region_5.6 | all-reduce | flops 1024 | bytes 8192 | tf_op jit(solution)/shard_map/psum | solution.py:76
  456.9 44.9 %all-reduce.9.cloned.1.call-done = f32[32,1024]{1,0:T(8,128)} async-done(((f32[32,1024]{1,0:T(8,128)}), f32[32,1024]{1,0:T(8,128)}) %all-reduce.9.cloned.1.call-update) | async-done | bytes 131088 | tf_op jit(solution)/shard_map/psum | solution.py:76
  501.8 1.2 convolution_divide_fusion
  503.0 0.9 fusion.19
  503.9 0.3 fusion.93
  504.2 280.1 %psum.63 = f32[32,32]{1,0:T(8,128)S(1)} all-reduce(f32[32,32]{1,0:T(8,128)S(1)} %fusion.93), channel_id=1, replica_groups=mesh['freq'=8,'tm'=64] {'tm'}, use_global_device_ids=true, to_apply=%region_7.8 | all-reduce | flops 1024 | bytes 8192 | tf_op jit(solution)/shard_map/psum | solution.py:82
  784.3 1.7 convolution_divide_fusion.2
  (15 shorter events, 0.2 us)
Async XLA Ops:
  7.2 142.1 %all-reduce.5.cloned.1.call-start = ((), (), s32[]{:S(2)}) async-start(), calls=%async_computation.1 | async-start | bytes 262144 | tf_op jit(solution)/shard_map/psum | solution.py:76
  51.4 24.1 %copy-start.1 = (f32[32,512]{1,0:T(8,128)S(1)}, f32[32,512]{1,0:T(8,128)}, u32[]{:S(2)}) copy-start(f32[32,512]{1,0:T(8,128)} %param.4) | copy-start | bytes 196612
  51.4 97.8 %copy-start.2 = (f32[32,1024]{1,0:T(8,128)S(1)}, f32[32,1024]{1,0:T(8,128)}, u32[]{:S(2)}) copy-start(f32[32,1024]{1,0:T(8,128)} %param.5) | copy-start | bytes 393220
  76.7 355.1 %all-reduce.7.cloned.1.call-start = ((), (), s32[]{:S(2)}) async-start(), calls=%async_computation.2 | async-start | bytes 131072 | tf_op jit(solution)/shard_map/psum | solution.py:82
  151.3 350.5 %all-reduce.9.cloned.1.call-start = ((), (), s32[]{:S(2)}) async-start(), calls=%async_computation.3 | async-start | bytes 262144 | tf_op jit(solution)/shard_map/psum | solution.py:76
  433.9 350.4 %all-reduce.11.cloned.1.call-start = ((), (), s32[]{:S(2)}) async-start(), calls=%async_computation.4 | async-start | bytes 131072 | tf_op jit(solution)/shard_map/psum | solution.py:82
  503.0 283.0 %copy-start = (f32[32,1024]{1,0:T(8,128)}, f32[32,1024]{1,0:T(8,128)S(1)}, u32[]{:S(2)}) copy-start(f32[32,1024]{1,0:T(8,128)S(1)} %convolution_divide_fusion) | copy-start | bytes 393220
Sparse Core Ops, SparseCore 0:
  76.8 72.4 all-reduce.4
  153.6 259.0 all-reduce.6
  434.0 67.7 all-reduce.8
  505.7 259.0 all-reduce.10
where the time goes:
time: 802 us; the launch traced here: 793 us
  blocking collectives  628 us (78%)
  waiting for transfers between devices  95.6 us (12%)
  matrix products  46.7 us (6%)
  between operations  14.1 us (2%)
    psum x2, blocking collectives, shards(): numer_w, gram_h = lax.psum((numer_w, gram_h), 'tm')  560 us
    psum x2, waiting for transfers between devices, shards(): numer_h, gram_w = lax.psum((numer_h, gram_w), 'freq')  95.5 us
    psum x2, blocking collectives, shards(): numer_h, gram_w = lax.psum((numer_h, gram_w), 'freq')  44.4 us
    all_to_all x1, blocking collectives, shards(): lax.all_to_all(magnitude, 'freq', split_axis=1, concat_axis=0, tiled=True)  22.9 us
  transfers between devices with their start and end apart: 4, of which 2 were waited for; matrix products, arithmetic and copies ran while one was open for 0% of the time, Pallas kernels for 0%

commit v1 on v0

v1 whole, which is shorter than its diff:
```python
import functools
import math

import jax
import jax.numpy as jnp
import ml_dtypes
import numpy as np
from jax import lax
from jax.experimental import pallas as pl
from jax.experimental.pallas import tpu as pltpu
from jax.sharding import PartitionSpec as P

MESH = pl.DeviceIdType.MESH
HIGHEST = lax.Precision.HIGHEST
F32 = jnp.float32
B16 = jnp.bfloat16

BINS = 4096
FRAME = 2 * BINS
ITERS = 2
COMP = 32
OUTER = 64
INNER = 128
NX, NY, NZ, NC = 4, 4, 16, 2
NF = NY * NC
NQ = NX * NY
OWN = BINS // NF
FRAMES = 128
GROUP = 16
GROUPS = FRAMES // GROUP
HALF_K = OUTER // 2
NK = HALF_K + 2
ROWS = COMP + 8
WROWS = COMP + 16


def two_terms(values):
    hi = values.astype(np.float32).astype(ml_dtypes.bfloat16)
    lo = (values - hi.astype(np.float64)).astype(np.float32).astype(ml_dtypes.bfloat16)
    return hi, lo


def tables():
    outer, inner, k = np.arange(OUTER), np.arange(INNER), np.arange(NK)
    angle = 2 * np.pi * (np.outer(k, outer) % OUTER) / OUTER
    first = np.zeros((2, NK, 8, 8, OUTER))
    for frame in range(8):
        first[0, :, frame, frame] = np.cos(angle)
        first[1, :, frame, frame] = -np.sin(angle)
    first_hi, first_lo = two_terms(first.reshape(2 * NK * 8, 8 * OUTER))
    angle = 2 * np.pi * np.outer(k, inner) / FRAME
    scale = 0.5 / math.sqrt(0.375 * FRAME)
    twist = np.stack([np.cos(angle) * scale, np.sin(angle) * scale])
    twist = np.concatenate([twist, twist], -1)[:, :, None, :]
    twist = np.ascontiguousarray(np.broadcast_to(twist, (2, NK, 8, 2 * INNER))).astype(np.float32)
    row = np.arange(INNER)
    second_k = np.where(row < 64, row, 191 - row)
    angle = 2 * np.pi * (np.outer(second_k, inner) % INNER) / INNER
    second_hi, second_lo = two_terms(
        np.block([[np.cos(angle), np.sin(angle)], [-np.sin(angle), np.cos(angle)]])
    )
    place = np.zeros((OWN, OWN), np.float32)
    for k1 in range(OUTER):
        at = k1 if k1 <= HALF_K else 3 * HALF_K - k1
        for k2 in range(8):
            place[OUTER * k2 + k1, at * 8 + k2] = 1.0
    return first_hi, first_lo, twist, second_hi, second_lo, place.astype(ml_dtypes.bfloat16)


def dot(a, b, precision=None):
    dims = (((1,), (0,)), ((), ()))
    return lax.dot_general(a, b, dims, precision=precision, preferred_element_type=F32)


def dot_t(a, b, precision=None):
    dims = (((1,), (1,)), ((), ()))
    return lax.dot_general(a, b, dims, precision=precision, preferred_element_type=F32)


def terms(value):
    hi = value.astype(B16)
    rest = value - hi.astype(F32)
    mid = rest.astype(B16)
    return hi, mid, (rest - mid.astype(F32)).astype(B16)


def pack(gram):
    return jnp.concatenate([gram[8 * i : 8 * i + 8] for i in range(4)], axis=1)


def unpack(tile):
    return jnp.concatenate([tile[:, 32 * i : 32 * i + 32] for i in range(4)], axis=0)


def gather_slot(block):
    tile = pack(dot_t(block, block, HIGHEST))
    hi = tile.astype(B16)
    lo = (tile - hi.astype(F32)).astype(B16)
    return jnp.concatenate([block.astype(B16), hi, lo], axis=0)


def first_stage(audio, first_hi, first_lo, twist, outer, g_hi, g_lo, g):
    span = 8 * FRAME
    start = pl.multiple_of(g * (2 * span), 2 * span)
    left = audio[:, pl.ds(start, span)].reshape(8 * OUTER, INNER)
    right = audio[:, pl.ds(start + span, span)].reshape(8 * OUTER, INNER)
    both = jnp.concatenate([left, right], axis=1)
    outer[...] = (dot(first_hi[...], both) + dot(first_lo[...], both)).reshape(outer.shape)
    frame = pl.multiple_of(g * GROUP, GROUP)

    def turned(k):
        re, im, c, s = outer[0, k], outer[1, k], twist[0, k], twist[1, k]
        return re * c + im * s, im * c - re * s

    def step(k, carry):
        before_re, before_im, re, im = carry
        after_re, after_im = turned(k + 1)
        out_re = re - 0.5 * (before_re + after_re)
        out_im = im - 0.5 * (before_im + after_im)
        value = jnp.concatenate(
            [
                jnp.concatenate([out_re[:, :INNER], out_im[:, :INNER]], axis=1),
                jnp.concatenate([out_re[:, INNER:], out_im[:, INNER:]], axis=1),
            ],
            axis=0,
        )
        hi = value.astype(B16)
        g_hi[k, pl.ds(frame, GROUP), :] = hi
        g_lo[k, pl.ds(frame, GROUP), :] = (value - hi.astype(F32)).astype(B16)
        return re, im, after_re, after_im

    zero_re, zero_im = turned(0)
    one_re, one_im = turned(1)
    lax.fori_loop(0, HALF_K + 1, step, (one_re, -one_im, zero_re, zero_im), unroll=3)


def second_stage(second_hi, second_lo, g_hi, g_lo, mag):
    def magnitudes(lhs_hi, lhs_lo, hi, lo):
        out = dot_t(lhs_hi, hi) + dot_t(lhs_hi, lo) + dot_t(lhs_lo, hi)
        half = out.shape[0] // 2
        re, im = out[:half], out[half:]
        return jnp.sqrt(re * re + im * im)

    def put(at, a, b):
        rows = jnp.concatenate([a.reshape(NF, 8, FRAMES), b.reshape(NF, 8, FRAMES)], axis=1)
        mag[:, pl.ds(pl.multiple_of(at * 8, 16), 16), :] = rows.astype(B16)

    def halves(ref):
        return jnp.concatenate([ref[0:64], ref[128:192]], axis=0)

    def pair(p):
        hi = g_hi[pl.ds(2 * p, 2)].reshape(2 * FRAMES, 2 * INNER)
        lo = g_lo[pl.ds(2 * p, 2)].reshape(2 * FRAMES, 2 * INNER)
        return magnitudes(second_hi[...], second_lo[...], hi, lo)

    middle = magnitudes(halves(second_hi), halves(second_lo), g_hi[HALF_K], g_lo[HALF_K])
    out = pair(0)
    put(0, out[:64, :FRAMES], out[:64, FRAMES:])
    put(HALF_K, middle, out[64:, FRAMES:])

    def step(p, _):
        out = pair(p)
        put(2 * p, out[:64, :FRAMES], out[:64, FRAMES:])
        put(HALF_K + 2 * p, out[64:, :FRAMES], out[64:, FRAMES:])
        return 0

    lax.fori_loop(1, HALF_K // 2, step, 0)


def kernel(
    audio_hbm, w_ref, h_ref, first_hi, first_lo, twist, second_hi, second_lo, place,
    w_out, h_out,
    audio, outer, g_hi, g_lo, mag,
    gathered, blocks, comp, act,
    send_core, recv_core, send_plane, recv_plane,
    send_z, recv_z, full_z, numer, gram_rows, last,
    audio_sem, gather_sem, core_sems, plane_sem, z_sem, full_sem, wide_sem, fwd_sem, last_sem, act_sem,
):
    f, t = lax.axis_index("freq"), lax.axis_index("tm")
    y, c = lax.div(f, NC), lax.rem(f, NC)
    z, x = lax.div(t, NX), lax.rem(t, NX)
    q = y * NX + x
    span = 16 * FRAME

    def signal(freq, tm):
        pl.semaphore_signal(
            pltpu.get_barrier_semaphore(), inc=1, device_id={"freq": freq, "tm": tm},
            device_id_type=MESH,
        )

    def remote(src, dst, sems, freq, tm):
        return pltpu.make_async_remote_copy(
            src_ref=src, dst_ref=dst, send_sem=sems.at[0], recv_sem=sems.at[1],
            device_id={"freq": freq, "tm": tm}, device_id_type=MESH,
        )

    def drain(ref, sem):
        pltpu.make_async_copy(ref, ref, sem).wait()

    def plane_peer(i):
        other = lax.rem(q + i, NQ)
        return NC * lax.div(other, NX) + c, NX * z + lax.rem(other, NX)

    def z_peer(i):
        return lax.rem(z + i, NZ)

    def load(g):
        part = pl.ds(pl.multiple_of(g * span, span), span)
        return pltpu.make_async_copy(audio_hbm.at[:, part], audio.at[:, part], audio_sem.at[g])

    def each(low, high, body):
        def step(i, _):
            body(i)
            return 0

        lax.fori_loop(low, high, step, 0)

    each(0, GROUPS, lambda g: load(g).start())

    def greet_plane(i):
        signal(*plane_peer(i))

    def greet_z(i):
        signal(f, NX * z_peer(i) + x)

    def greet_other(i):
        signal(NC * i + (1 - c), t)

    each(1, NQ, greet_plane)
    each(1, NZ, greet_z)
    each(0, NY, greet_other)

    spread = dot(jnp.concatenate(terms(w_ref[...]), axis=0), place[...])
    spread = spread[:COMP] + spread[COMP : 2 * COMP] + spread[2 * COMP :]
    mine = c * NQ + y * NX
    for j in range(NX):
        block = spread[:, 128 * j : 128 * j + 128]
        blocks[j] = block
        gathered[0, mine + j] = gather_slot(block)
    comp[...] = blocks[x]
    act[...] = h_ref[:, pl.ds(pl.multiple_of(f * FRAMES, FRAMES), FRAMES)]

    def spectra(g):
        load(g).wait()
        first_stage(audio, first_hi, first_lo, twist, outer, g_hi, g_lo, g)

    each(0, GROUPS, spectra)

    pl.semaphore_wait(pltpu.get_barrier_semaphore(), (NQ - 1) + (NZ - 1) + NY)

    def send_start(i):
        slots = gathered.at[0, pl.ds(mine, NX)]
        remote(slots, slots, gather_sem, lax.rem(f + i, NF), t).start()

    each(1, NF, send_start)
    second_stage(second_hi, second_lo, g_hi, g_lo, mag)
    drain(gathered.at[0, pl.ds(0, (NF - 1) * NX)], gather_sem.at[1])

    for it in range(ITERS):
        def product(core):
            total = jnp.zeros((COMP, FRAMES), F32)
            for yy in range(NY):
                first = core * NQ + yy * NX
                rows = [gathered[it, first + j, :COMP, :] for j in range(NX)]
                total += dot(jnp.concatenate(rows, axis=1), mag[NC * yy + core])
            return total

        def gram_of(core):
            def add(i, total):
                tile = gathered[it, core * NQ + i, COMP:, :].astype(F32)
                return total + (tile[:8] + tile[8:])

            return lax.fori_loop(0, NQ, add, jnp.zeros((8, 128), F32), unroll=4)

        numer_h = product(c)
        gram_w = gram_of(c)
        if it == 1:
            drain(gathered.at[1, pl.ds(0, NQ)], fwd_sem.at[1])
        numer_h += product(1 - c)
        gram_w = unpack(gram_w + gram_of(1 - c))
        state = act[...]
        state = state * numer_h / dot(gram_w, state, HIGHEST)
        act[...] = state
        rounded = state.astype(B16)
        gram_h = pack(dot_t(state, state, HIGHEST))

        core_sem = core_sems.at[it]
        order = (2, 1, 3, 0)

        def partial(freq):
            return dot_t(rounded, mag[freq])

        for step, dy in enumerate(order):
            yy = lax.rem(y + dy, NY)
            value = partial(NC * yy + (1 - c))
            for j in range(NX):
                tile = jnp.concatenate([value[:, 128 * j : 128 * j + 128], gram_h], axis=0)
                send_core[it, yy * NX + j] = tile
            slots = pl.ds(yy * NX, NX)
            remote(
                send_core.at[it, slots], recv_core.at[it, slots], core_sem.at[step],
                NC * y + (1 - c), t,
            ).start()
        for step, dy in enumerate(order):
            yy = lax.rem(y + dy, NY)
            value = partial(NC * yy + c)
            drain(recv_core.at[it, pl.ds(yy * NX, NX)], core_sem.at[step, 1])
            for j in range(NX):
                slot = yy * NX + j
                tile = jnp.concatenate([value[:, 128 * j : 128 * j + 128], gram_h], axis=0)
                send_plane[it, slot] = tile + recv_core[it, slot]
            for dx in range(NX):
                xx = lax.rem(x + dx, NX)
                slot = yy * NX + xx
                if dy == 0 and dx == 0:
                    recv_plane[it, q] = send_plane[it, q]
                else:
                    remote(
                        send_plane.at[it, slot], recv_plane.at[it, q], plane_sem.at[it],
                        NC * yy + c, NX * z + xx,
                    ).start()

        if it == ITERS - 1:
            columns = pl.ds(pl.multiple_of(f * FRAMES, FRAMES), FRAMES)
            h_out[:, columns] = state

            def send_act(i):
                remote(act, h_out.at[:, columns], act_sem, lax.rem(f + i, NF), t).start()

            each(1, NF, send_act)

        drain(recv_plane.at[it, pl.ds(0, NQ - 1)], plane_sem.at[it, 1])
        total = recv_plane[it, 0]
        for i in range(1, NQ):
            total += recv_plane[it, i]
        for i in range(NZ):
            row = total[COMP + i // 2 : COMP + i // 2 + 1]
            send_z[it, i] = jnp.concatenate([total[2 * i : 2 * i + 2], row, row], axis=0)
        recv_z[it, z] = send_z[it, z]

        def scatter(i):
            zz = z_peer(i)
            remote(send_z.at[it, zz], recv_z.at[it, z], z_sem.at[it], f, NX * zz + x).start()

        each(1, NZ, scatter)
        drain(recv_z.at[it, pl.ds(0, NZ - 1)], z_sem.at[it, 1])
        part = recv_z[it, 0]
        for i in range(1, NZ):
            part += recv_z[it, i]
        full_z[it, z] = part

        def share(i):
            own = full_z.at[it, z]
            remote(own, own, full_sem.at[it], f, NX * z_peer(i) + x).start()

        each(1, NZ, share)
        drain(full_z.at[it, pl.ds(0, NZ - 1)], full_sem.at[it, 1])
        for i in range(NZ):
            numer[2 * i : 2 * i + 2, :] = full_z[it, i, 0:2, :]
            if i % 2 == 0:
                gram_rows[i // 2 : i // 2 + 1, :] = full_z[it, i, 2:3, :]
        own = comp[...]
        own = own * numer[...] / dot(unpack(gram_rows[...]), own, HIGHEST)
        comp[...] = own

        if it < ITERS - 1:
            at = c * NQ + q
            gathered[it + 1, at] = gather_slot(own)

            def spread_plane(i):
                slot = gathered.at[it + 1, at]
                remote(slot, slot, wide_sem, *plane_peer(i)).start()

            each(1, NQ, spread_plane)
            drain(gathered.at[it + 1, pl.ds(0, NQ - 1)], wide_sem.at[1])
            slots = gathered.at[it + 1, pl.ds(c * NQ, NQ)]
            remote(slots, slots, fwd_sem, NC * y + (1 - c), t).start()
        else:
            last[x] = own

            def spread_x(i):
                remote(comp, last.at[x], last_sem, f, NX * z + lax.rem(x + i, NX)).start()

            each(1, NX, spread_x)
            drain(last.at[pl.ds(0, NX - 1)], last_sem.at[1])

    whole = jnp.concatenate([last[j] for j in range(NX)], axis=1)
    whole = dot_t(jnp.concatenate(terms(whole), axis=0), place[...])
    w_out[...] = whole[:COMP] + whole[COMP : 2 * COMP] + whole[2 * COMP :]

    drain(h_out.at[:, pl.ds(0, (NF - 1) * FRAMES)], act_sem.at[1])
    drain(h_out.at[:, pl.ds(0, (NF - 1) * FRAMES)], act_sem.at[0])
    drain(gathered.at[0, pl.ds(0, (NF - 1) * NX)], gather_sem.at[0])
    drain(gathered.at[1, pl.ds(0, NQ - 1)], wide_sem.at[0])
    drain(gathered.at[1, pl.ds(0, NQ)], fwd_sem.at[0])
    drain(last.at[pl.ds(0, NX - 1)], last_sem.at[0])
    for it in range(ITERS):
        for step in range(NY):
            drain(send_core.at[it, pl.ds(0, NX)], core_sems.at[it, step, 0])
        drain(send_plane.at[it, pl.ds(0, NQ - 1)], plane_sem.at[it, 0])
        drain(send_z.at[it, pl.ds(0, NZ - 1)], z_sem.at[it, 0])
        drain(full_z.at[it, pl.ds(0, NZ - 1)], full_sem.at[it, 0])


def shards(audio, w_start, h_start):
    vmem = pl.BlockSpec(memory_space=pltpu.VMEM)
    dma = pltpu.SemaphoreType.DMA
    constants = [jnp.asarray(table) for table in tables()]
    return pl.pallas_call(
        kernel,
        out_shape=(
            jax.ShapeDtypeStruct((COMP, OWN), F32),
            jax.ShapeDtypeStruct((COMP, NF * FRAMES), F32),
        ),
        in_specs=[pl.BlockSpec(memory_space=pl.ANY)] + [vmem] * (2 + len(constants)),
        out_specs=(vmem, vmem),
        scratch_shapes=[
            pltpu.VMEM((1, FRAMES * FRAME), B16),
            pltpu.VMEM((2, NK, 8, 2 * INNER), F32),
            pltpu.VMEM((HALF_K + 1, FRAMES, 2 * INNER), B16),
            pltpu.VMEM((HALF_K + 1, FRAMES, 2 * INNER), B16),
            pltpu.VMEM((NF, OWN, FRAMES), B16),
            pltpu.VMEM((ITERS, NC * NQ, WROWS, 128), B16),
            pltpu.VMEM((NX, COMP, 128), F32),
            pltpu.VMEM((COMP, 128), F32),
            pltpu.VMEM((COMP, FRAMES), F32),
            pltpu.VMEM((ITERS, NQ, ROWS, 128), F32),
            pltpu.VMEM((ITERS, NQ, ROWS, 128), F32),
            pltpu.VMEM((ITERS, NQ, ROWS, 128), F32),
            pltpu.VMEM((ITERS, NQ, ROWS, 128), F32),
            pltpu.VMEM((ITERS, NZ, 4, 128), F32),
            pltpu.VMEM((ITERS, NZ, 4, 128), F32),
            pltpu.VMEM((ITERS, NZ, 4, 128), F32),
            pltpu.VMEM((COMP, 128), F32),
            pltpu.VMEM((8, 128), F32),
            pltpu.VMEM((NX, COMP, 128), F32),
            dma((GROUPS,)),
            dma((2,)),
            dma((ITERS, NY, 2)),
            dma((ITERS, 2)),
            dma((ITERS, 2)),
            dma((ITERS, 2)),
            dma((2,)),
            dma((2,)),
            dma((2,)),
            dma((2,)),
        ],
        compiler_params=pltpu.CompilerParams(
            collective_id=0, has_side_effects=True, vmem_limit_bytes=50 * 2**20
        ),
    )(audio, w_start, h_start, *constants)


def solution(mesh):
    placed = (P("tm", "freq"), P(None, "freq"), P(None, "tm"))
    return jax.shard_map(
        shards,
        mesh=mesh,
        in_specs=placed,
        out_specs=(P(None, "freq"), P(None, "tm")),
        check_vma=False,
    )
```

time: 802 us -> 89.7 us (0.11)
  the two profiles are of different devices: /device:TPU:8 before, /device:TPU:6 now
where the time goes in v1:
time: 89.7 us; the launch traced here: 88.4 us
  Pallas kernels  78.7 us (88%)
  local copies, waits for them, and re-layouts  9.03 us (10%)
    pallas_call x1, Pallas kernels, shards(): pl.pallas_call(kernel, out_shape=(jax.ShapeDtypeStruct((COMP, OWN), F32),...  78.7 us
    unnamed x18, local copies, waits for them, and re-layouts  9.03 us

profile of v1, /device:TPU:6, one launch (start us, length us, event | category | flops | bytes accessed | tf_op | source)
XLA Modules:
  0.0 88.4 jit_solution(2067149438815704259)
XLA Ops:
  0.6 0.0 copy-start
  0.6 1.0 %copy-done = f32[2,34,8,256]{3,2,1,0:T(8,128)S(1)} copy-done((f32[2,34,8,256]{3,2,1,0:T(8,128)S(1)}, f32[2,34,8,256]{3,2,1,0:T(8,128)}, u32[]{:S(2)}) %copy-start) | copy-done | bytes 557080
  1.7 0.0 copy-start.1
  1.7 1.1 %copy-done.1 = bf16[544,512]{1,0:T(8,128)(2,1)S(1)} copy-done((bf16[544,512]{1,0:T(8,128)(2,1)S(1)}, bf16[544,512]{1,0:T(8,128)(2,1)}, u32[]{:S(2)}) %copy-start.1) | copy-done | bytes 557080
  2.7 0.0 copy-start.2
  2.7 1.1 %copy-done.2 = bf16[544,512]{1,0:T(8,128)(2,1)S(1)} copy-done((bf16[544,512]{1,0:T(8,128)(2,1)S(1)}, bf16[544,512]{1,0:T(8,128)(2,1)}, u32[]{:S(2)}) %copy-start.2) | copy-done | bytes 557080
  3.8 0.0 copy-start.3
  3.8 1.0 %copy-done.3 = bf16[512,512]{1,0:T(8,128)(2,1)S(1)} copy-done((bf16[512,512]{1,0:T(8,128)(2,1)S(1)}, bf16[512,512]{1,0:T(8,128)(2,1)}, u32[]{:S(2)}) %copy-start.3) | copy-done | bytes 524312
  4.8 0.0 copy-start.4
  4.8 0.9 %copy-done.4 = f32[32,1024]{1,0:T(8,128)S(1)} copy-done((f32[32,1024]{1,0:T(8,128)S(1)}, f32[32,1024]{1,0:T(8,128)}, u32[]{:S(2)}) %copy-start.4) | copy-done | bytes 131096
  5.7 0.0 copy-start.5
  5.7 0.9 %copy-done.5 = bf16[256,256]{1,0:T(8,128)(2,1)S(1)} copy-done((bf16[256,256]{1,0:T(8,128)(2,1)S(1)}, bf16[256,256]{1,0:T(8,128)(2,1)}, u32[]{:S(2)}) %copy-start.5) | copy-done | bytes 131096
  6.6 0.0 copy-start.6
  6.6 0.9 %copy-done.6 = bf16[256,256]{1,0:T(8,128)(2,1)S(1)} copy-done((bf16[256,256]{1,0:T(8,128)(2,1)S(1)}, bf16[256,256]{1,0:T(8,128)(2,1)}, u32[]{:S(2)}) %copy-start.6) | copy-done | bytes 131096
  7.6 0.0 copy-start.7
  7.6 0.8 copy-done.7
  8.4 78.7 %shard_map.104 = (f32[32,512]{1,0:T(8,128)S(1)}, f32[32,1024]{1,0:T(8,128)S(1)}) custom-call(bf16[1,1048576]{1,0:T(2,128)(2,1)} %audio_hbm.1, f32[32,512]{1,0:T(8,128)S(1)} %copy-done.7, f32[32,1024]{1,0:T(8,128)S(1)} %copy-done.4, bf16[544,512]{1,0:T(8,128)(2,1)S(1)} %copy-done.2, bf16[544,512]{1,0:T(8,128)(2,1)S(1)} %copy-done.1, ...), custom_call_target="tpu_custom_call" | custom-call | tf_op jit(solution)/shard_map/pallas_call | solution.py:409
  87.1 0.6 copy.13
  87.7 0.7 copy.14
Async XLA Ops:
  0.6 1.1 %copy-start = (f32[2,34,8,256]{3,2,1,0:T(8,128)S(1)}, f32[2,34,8,256]{3,2,1,0:T(8,128)}, u32[]{:S(2)}) copy-start(f32[2,34,8,256]{3,2,1,0:T(8,128)} %constant.14.clone.twist) | copy-start | bytes 1671172
  1.7 1.1 %copy-start.1 = (bf16[544,512]{1,0:T(8,128)(2,1)S(1)}, bf16[544,512]{1,0:T(8,128)(2,1)}, u32[]{:S(2)}) copy-start(bf16[544,512]{1,0:T(8,128)(2,1)} %constant.13.clone.first_lo) | copy-start | bytes 1671172
  2.7 1.1 %copy-start.2 = (bf16[544,512]{1,0:T(8,128)(2,1)S(1)}, bf16[544,512]{1,0:T(8,128)(2,1)}, u32[]{:S(2)}) copy-start(bf16[544,512]{1,0:T(8,128)(2,1)} %constant.12.clone.first_hi) | copy-start | bytes 1671172
  3.8 1.0 %copy-start.3 = (bf16[512,512]{1,0:T(8,128)(2,1)S(1)}, bf16[512,512]{1,0:T(8,128)(2,1)}, u32[]{:S(2)}) copy-start(bf16[512,512]{1,0:T(8,128)(2,1)} %constant.17.clone.place) | copy-start | bytes 1572868
  4.8 0.9 %copy-start.4 = (f32[32,1024]{1,0:T(8,128)S(1)}, f32[32,1024]{1,0:T(8,128)}, u32[]{:S(2)}) copy-start(f32[32,1024]{1,0:T(8,128)} %h_ref.1) | copy-start | bytes 393220
  5.7 0.9 %copy-start.5 = (bf16[256,256]{1,0:T(8,128)(2,1)S(1)}, bf16[256,256]{1,0:T(8,128)(2,1)}, u32[]{:S(2)}) copy-start(bf16[256,256]{1,0:T(8,128)(2,1)} %constant.16.clone.second_lo) | copy-start | bytes 393220
  6.6 0.9 %copy-start.6 = (bf16[256,256]{1,0:T(8,128)(2,1)S(1)}, bf16[256,256]{1,0:T(8,128)(2,1)}, u32[]{:S(2)}) copy-start(bf16[256,256]{1,0:T(8,128)(2,1)} %constant.15.clone.second_hi) | copy-start | bytes 393220
  7.6 0.8 copy-start.7

commit v2 on v1

--- a/solution.py
+++ b/solution.py
@@ -31,7 +31,9 @@
 HALF_K = OUTER // 2
 NK = HALF_K + 2
 ROWS = COMP + 8
-WROWS = COMP + 16
+PACKED = COMP // 2 + 8
+NS = 2 * NQ
+HALF = 64
 
 
 def two_terms(values):
@@ -92,11 +94,14 @@
     return jnp.concatenate([tile[:, 32 * i : 32 * i + 32] for i in range(4)], axis=0)
 
 
-def gather_slot(block):
-    tile = pack(dot_t(block, block, HIGHEST))
-    hi = tile.astype(B16)
-    lo = (tile - hi.astype(F32)).astype(B16)
-    return jnp.concatenate([block.astype(B16), hi, lo], axis=0)
+def swap(value):
+    return jnp.concatenate([value[:, HALF:], value[:, :HALF]], axis=1)
+
+
+def gather_slot(mine, block, gram):
+    hi = gram.astype(B16).astype(F32)
+    both = jnp.concatenate([hi, gram - hi], axis=1)
+    return jnp.where(mine, block, jnp.concatenate([both, both], axis=1)).astype(B16)
 
 
 def first_stage(audio, first_hi, first_lo, twist, outer, g_hi, g_lo, g):
@@ -168,18 +173,21 @@
 
 
 def kernel(
-    audio_hbm, w_ref, h_ref, first_hi, first_lo, twist, second_hi, second_lo, place,
+    audio_hbm, w_hbm, h_hbm, first_hi_hbm, first_lo_hbm, twist_hbm, second_hi_hbm, second_lo_hbm,
+    place_hbm,
     w_out, h_out,
-    audio, outer, g_hi, g_lo, mag,
-    gathered, blocks, comp, act,
-    send_core, recv_core, send_plane, recv_plane,
-    send_z, recv_z, full_z, numer, gram_rows, last,
-    audio_sem, gather_sem, core_sems, plane_sem, z_sem, full_sem, wide_sem, fwd_sem, last_sem, act_sem,
+    audio, w_in, h_in, first_hi, first_lo, twist, second_hi, second_lo, place,
+    outer, g_hi, g_lo, mag,
+    gathered, comp, act,
+    send_core, recv_core, send_plane, recv_plane, sums, last,
+    audio_sem, load_sem, gather_sem, core_sems, plane_sem, z_sem, wide_sem, fwd_sem, last_sem, act_sem,
 ):
     f, t = lax.axis_index("freq"), lax.axis_index("tm")
     y, c = lax.div(f, NC), lax.rem(f, NC)
     z, x = lax.div(t, NX), lax.rem(t, NX)
+    far, m = lax.div(z, 2), lax.rem(z, 2)
     q = y * NX + x
+    own_slot = 2 * q + m
     span = 16 * FRAME
 
     def signal(freq, tm):
@@ -197,16 +205,39 @@
     def drain(ref, sem):
         pltpu.make_async_copy(ref, ref, sem).wait()
 
-    def plane_peer(i):
-        other = lax.rem(q + i, NQ)
-        return NC * lax.div(other, NX) + c, NX * z + lax.rem(other, NX)
-
-    def z_peer(i):
-        return lax.rem(z + i, NZ)
-
-    def load(g):
+    def slot_device(slot):
+        chip = lax.div(slot, 2)
+        zz = z - m + lax.rem(slot, 2)
+        return NC * lax.div(chip, NX) + c, NX * zz + lax.rem(chip, NX)
+
+    def near_peer(i):
+        return slot_device(lax.rem(own_slot + i, NS))
+
+    def far_peer(i):
+        return f, NX * (2 * lax.rem(far + i, NZ // 2) + m) + x
+
+    def load_audio(g):
         part = pl.ds(pl.multiple_of(g * span, span), span)
         return pltpu.make_async_copy(audio_hbm.at[:, part], audio.at[:, part], audio_sem.at[g])
+
+    def load(src, dst, i):
+        return pltpu.make_async_copy(src, dst, load_sem.at[i])
+
+    loads = [
+        load(src, dst, i)
+        for i, (src, dst) in enumerate(
+            (
+                (first_hi_hbm, first_hi),
+                (first_lo_hbm, first_lo),
+                (twist_hbm, twist),
+                (w_hbm, w_in),
+                (place_hbm, place),
+                (second_hi_hbm, second_hi),
+                (second_lo_hbm, second_lo),
+                (h_hbm, h_in),
+            )
+        )
+    ]
 
     def each(low, high, body):
         def step(i, _):
@@ -215,69 +246,78 @@
 
         lax.fori_loop(low, high, step, 0)
 
-    each(0, GROUPS, lambda g: load(g).start())
-
-    def greet_plane(i):
-        signal(*plane_peer(i))
-
-    def greet_z(i):
-        signal(f, NX * z_peer(i) + x)
-
-    def greet_other(i):
-        signal(NC * i + (1 - c), t)
-
-    each(1, NQ, greet_plane)
-    each(1, NZ, greet_z)
-    each(0, NY, greet_other)
-
-    spread = dot(jnp.concatenate(terms(w_ref[...]), axis=0), place[...])
+    load_audio(0).start()
+    for copy in loads[:3]:
+        copy.start()
+    each(1, NZ // 2, lambda i: signal(*far_peer(i)))
+    each(1, NS, lambda i: signal(*near_peer(i)))
+    each(0, NY, lambda i: signal(NC * i + (1 - c), t))
+    each(1, GROUPS, lambda g: load_audio(g).start())
+    for copy in loads[3:]:
+        copy.start()
+    for copy in loads[:3]:
+        copy.wait()
+
+    def spectra(g):
+        load_audio(g).wait()
+        first_stage(audio, first_hi, first_lo, twist, outer, g_hi, g_lo, g)
+
+    each(0, GROUPS, spectra)
+
+    for copy in loads[3:]:
+        copy.wait()
+    lane = lax.broadcasted_iota(jnp.int32, (COMP, 128), 1)
+    low = lane < HALF
+    mine = lax.div(lane, HALF) == m
+    spread = dot(jnp.concatenate(terms(w_in[...]), axis=0), place[...])
     spread = spread[:COMP] + spread[COMP : 2 * COMP] + spread[2 * COMP :]
-    mine = c * NQ + y * NX
+    gram = dot_t(spread, spread, HIGHEST)
+    none = jnp.zeros_like(gram)
+    first_slot = c * NS + 2 * NX * y
     for j in range(NX):
         block = spread[:, 128 * j : 128 * j + 128]
-        blocks[j] = block
-        gathered[0, mine + j] = gather_slot(block)
-    comp[...] = blocks[x]
-    act[...] = h_ref[:, pl.ds(pl.multiple_of(f * FRAMES, FRAMES), FRAMES)]
-
-    def spectra(g):
-        load(g).wait()
-        first_stage(audio, first_hi, first_lo, twist, outer, g_hi, g_lo, g)
-
-    each(0, GROUPS, spectra)
-
-    pl.semaphore_wait(pltpu.get_barrier_semaphore(), (NQ - 1) + (NZ - 1) + NY)
+        last[2 * j] = block
+        gathered[0, first_slot + 2 * j] = gather_slot(low, block, gram if j == 0 else none)
+        gathered[0, first_slot + 2 * j + 1] = gather_slot(lane >= HALF, block, none)
+    comp[...] = last[2 * x]
+    act[...] = h_in[:, pl.ds(pl.multiple_of(f * FRAMES, FRAMES), FRAMES)]
+
+    pl.semaphore_wait(pltpu.get_barrier_semaphore(), (NS - 1) + (NZ // 2 - 1) + NY)
 
     def send_start(i):
-        slots = gathered.at[0, pl.ds(mine, NX)]
+        slots = gathered.at[0, pl.ds(first_slot, 2 * NX)]
         remote(slots, slots, gather_sem, lax.rem(f + i, NF), t).start()
 
     each(1, NF, send_start)
     second_stage(second_hi, second_lo, g_hi, g_lo, mag)
-    drain(gathered.at[0, pl.ds(0, (NF - 1) * NX)], gather_sem.at[1])
+    drain(gathered.at[0, pl.ds(0, (NF - 1) * 2 * NX)], gather_sem.at[1])
 
     for it in range(ITERS):
         def product(core):
             total = jnp.zeros((COMP, FRAMES), F32)
             for yy in range(NY):
-                first = core * NQ + yy * NX
-                rows = [gathered[it, first + j, :COMP, :] for j in range(NX)]
+                first = core * NS + 2 * NX * yy
+                rows = [
+                    jnp.where(low, gathered[it, first + 2 * j], gathered[it, first + 2 * j + 1])
+                    for j in range(NX)
+                ]
                 total += dot(jnp.concatenate(rows, axis=1), mag[NC * yy + core])
             return total
 
         def gram_of(core):
             def add(i, total):
-                tile = gathered[it, core * NQ + i, COMP:, :].astype(F32)
-                return total + (tile[:8] + tile[8:])
-
-            return lax.fori_loop(0, NQ, add, jnp.zeros((8, 128), F32), unroll=4)
+                at = core * NS + 2 * i
+                return total + jnp.where(low, gathered[it, at + 1], gathered[it, at]).astype(F32)
+
+            return lax.fori_loop(0, NQ, add, jnp.zeros((COMP, 128), F32), unroll=4)
 
         numer_h = product(c)
         gram_w = gram_of(c)
         if it == 1:
-            drain(gathered.at[1, pl.ds(0, NQ)], fwd_sem.at[1])
+            drain(gathered.at[1, pl.ds(0, NS)], fwd_sem.at[1])
         numer_h += product(1 - c)
-        gram_w = unpack(gram_w + gram_of(1 - c))
+        gram_w += gram_of(1 - c)
+        gram_w = (gram_w[:, :32] + gram_w[:, 64:96]) + (gram_w[:, 32:64] + gram_w[:, 96:])
         state = act[...]
         state = state * numer_h / dot(gram_w, state, HIGHEST)
         act[...] = state
@@ -306,19 +346,25 @@
             value = partial(NC * yy + c)
             drain(recv_core.at[it, pl.ds(yy * NX, NX)], core_sem.at[step, 1])
             for j in range(NX):
-                slot = yy * NX + j
+                chip = yy * NX + j
                 tile = jnp.concatenate([value[:, 128 * j : 128 * j + 128], gram_h], axis=0)
-                send_plane[it, slot] = tile + recv_core[it, slot]
+                tile += recv_core[it, chip]
+                top, bottom, sum_h = tile[:16], tile[16:32], tile[32:]
+                left = jnp.where(low[:16], top, swap(bottom))
+                right = jnp.where(low[:16], swap(top), bottom)
+                send_plane[it, 2 * chip] = jnp.concatenate([left, sum_h], axis=0)
+                send_plane[it, 2 * chip + 1] = jnp.concatenate([right, sum_h], axis=0)
             for dx in range(NX):
                 xx = lax.rem(x + dx, NX)
-                slot = yy * NX + xx
-                if dy == 0 and dx == 0:
-                    recv_plane[it, q] = send_plane[it, q]
-                else:
-                    remote(
-                        send_plane.at[it, slot], recv_plane.at[it, q], plane_sem.at[it],
-                        NC * yy + c, NX * z + xx,
-                    ).start()
+                for dm in range(2):
+                    slot = 2 * (yy * NX + xx) + lax.rem(m + dm, 2)
+                    if dy == 0 and dx == 0 and dm == 0:
+                        recv_plane[it, own_slot] = send_plane[it, own_slot]
+                    else:
+                        remote(
+                            send_plane.at[it, slot], recv_plane.at[it, own_slot],
+                            plane_sem.at[it], *slot_device(slot),
+                        ).start()
 
         if it == ITERS - 1:
             columns = pl.ds(pl.multiple_of(f * FRAMES, FRAMES), FRAMES)
@@ -329,115 +375,105 @@
 
             each(1, NF, send_act)
 
-        drain(recv_plane.at[it, pl.ds(0, NQ - 1)], plane_sem.at[it, 1])
+        drain(recv_plane.at[it, pl.ds(0, NS - 1)], plane_sem.at[it, 1])
         total = recv_plane[it, 0]
-        for i in range(1, NQ):
+        for i in range(1, NS):
             total += recv_plane[it, i]
-        for i in range(NZ):
-            row = total[COMP + i // 2 : COMP + i // 2 + 1]
-            send_z[it, i] = jnp.concatenate([total[2 * i : 2 * i + 2], row, row], axis=0)
-        recv_z[it, z] = send_z[it, z]
-
-        def scatter(i):
-            zz = z_peer(i)
-            remote(send_z.at[it, zz], recv_z.at[it, z], z_sem.at[it], f, NX * zz + x).start()
-
-        each(1, NZ, scatter)
-        drain(recv_z.at[it, pl.ds(0, NZ - 1)], z_sem.at[it, 1])
-        part = recv_z[it, 0]
-        for i in range(1, NZ):
-            part += recv_z[it, i]
-        full_z[it, z] = part
+        sums[it, far] = total
 
         def share(i):
-            own = full_z.at[it, z]
-            remote(own, own, full_sem.at[it], f, NX * z_peer(i) + x).start()
-
-        each(1, NZ, share)
-        drain(full_z.at[it, pl.ds(0, NZ - 1)], full_sem.at[it, 1])
-        for i in range(NZ):
-            numer[2 * i : 2 * i + 2, :] = full_z[it, i, 0:2, :]
-            if i % 2 == 0:
-                gram_rows[i // 2 : i // 2 + 1, :] = full_z[it, i, 2:3, :]
+            own = sums.at[it, far]
+            remote(own, own, z_sem.at[it], *far_peer(i)).start()
+
+        each(1, NZ // 2, share)
+        drain(sums.at[it, pl.ds(0, NZ // 2 - 1)], z_sem.at[it, 1])
+        total = sums[it, 0]
+        for i in range(1, NZ // 2):
+            total += sums[it, i]
+        packed = total[:16]
+        other = swap(packed)
+        numer_w = jnp.concatenate(
+            [jnp.where(m == 0, packed, other), jnp.where(m == 0, other, packed)], axis=0
+        )
         own = comp[...]
-        own = own * numer[...] / dot(unpack(gram_rows[...]), own, HIGHEST)
+        below = dot(unpack(total[16:]), own, HIGHEST)
+        own = jnp.where(mine, own * numer_w / jnp.where(mine, below, 1.0), 0.0)
         comp[...] = own
 
         if it < ITERS - 1:
-            at = c * NQ + q
-            gathered[it + 1, at] = gather_slot(own)
-
-            def spread_plane(i):
+            at = c * NS + own_slot
+            gathered[it + 1, at] = gather_slot(mine, own, dot_t(own, own, HIGHEST))
+
+            def spread_near(i):
                 slot = gathered.at[it + 1, at]
-                remote(slot, slot, wide_sem, *plane_peer(i)).start()
-
-            each(1, NQ, spread_plane)
-            drain(gathered.at[it + 1, pl.ds(0, NQ - 1)], wide_sem.at[1])
-            slots = gathered.at[it + 1, pl.ds(c * NQ, NQ)]
+                remote(slot, slot, wide_sem, *near_peer(i)).start()
+
+            each(1, NS, spread_near)
+            drain(gathered.at[it + 1, pl.ds(0, NS - 1)], wide_sem.at[1])
+            slots = gathered.at[it + 1, pl.ds(c * NS, NS)]
             remote(slots, slots, fwd_sem, NC * y + (1 - c), t).start()
         else:
-            last[x] = own
+            end = 2 * x + m
+            last[end] = own
 
             def spread_x(i):
-                remote(comp, last.at[x], last_sem, f, NX * z + lax.rem(x + i, NX)).start()
-
-            each(1, NX, spread_x)
-            drain(last.at[pl.ds(0, NX - 1)], last_sem.at[1])
-
-    whole = jnp.concatenate([last[j] for j in range(NX)], axis=1)
+                peer = lax.rem(end + i, 2 * NX)
+                zz = z - m + lax.rem(peer, 2)
+                remote(comp, last.at[end], last_sem, f, NX * zz + lax.div(peer, 2)).start()
+
+            each(1, 2 * NX, spread_x)
+            drain(last.at[pl.ds(0, 2 * NX - 1)], last_sem.at[1])
+
+    whole = [jnp.where(low, last[2 * j], last[2 * j + 1]) for j in range(NX)]
+    whole = jnp.concatenate(whole, axis=1)
     whole = dot_t(jnp.concatenate(terms(whole), axis=0), place[...])
     w_out[...] = whole[:COMP] + whole[COMP : 2 * COMP] + whole[2 * COMP :]
 
     drain(h_out.at[:, pl.ds(0, (NF - 1) * FRAMES)], act_sem.at[1])
     drain(h_out.at[:, pl.ds(0, (NF - 1) * FRAMES)], act_sem.at[0])
-    drain(gathered.at[0, pl.ds(0, (NF - 1) * NX)], gather_sem.at[0])
-    drain(gathered.at[1, pl.ds(0, NQ - 1)], wide_sem.at[0])
-    drain(gathered.at[1, pl.ds(0, NQ)], fwd_sem.at[0])
-    drain(last.at[pl.ds(0, NX - 1)], last_sem.at[0])
+    drain(gathered.at[0, pl.ds(0, (NF - 1) * 2 * NX)], gather_sem.at[0])
+    drain(gathered.at[1, pl.ds(0, NS - 1)], wide_sem.at[0])
+    drain(gathered.at[1, pl.ds(0, NS)], fwd_sem.at[0])
+    drain(last.at[pl.ds(0, 2 * NX - 1)], last_sem.at[0])
     for it in range(ITERS):
         for step in range(NY):
             drain(send_core.at[it, pl.ds(0, NX)], core_sems.at[it, step, 0])
-        drain(send_plane.at[it, pl.ds(0, NQ - 1)], plane_sem.at[it, 0])
-        drain(send_z.at[it, pl.ds(0, NZ - 1)], z_sem.at[it, 0])
-        drain(full_z.at[it, pl.ds(0, NZ - 1)], full_sem.at[it, 0])
+        drain(send_plane.at[it, pl.ds(0, NS - 1)], plane_sem.at[it, 0])
+        drain(sums.at[it, pl.ds(0, NZ // 2 - 1)], z_sem.at[it, 0])
 
 
 def shards(audio, w_start, h_start):
     vmem = pl.BlockSpec(memory_space=pltpu.VMEM)
     dma = pltpu.SemaphoreType.DMA
     constants = [jnp.asarray(table) for table in tables()]
+    operands = (audio, w_start, h_start, *constants)
     return pl.pallas_call(
         kernel,
         out_shape=(
             jax.ShapeDtypeStruct((COMP, OWN), F32),
             jax.ShapeDtypeStruct((COMP, NF * FRAMES), F32),
         ),
-        in_specs=[pl.BlockSpec(memory_space=pl.ANY)] + [vmem] * (2 + len(constants)),
+        in_specs=[pl.BlockSpec(memory_space=pltpu.HBM)] * len(operands),
         out_specs=(vmem, vmem),
         scratch_shapes=[
-            pltpu.VMEM((1, FRAMES * FRAME), B16),
+            *(pltpu.VMEM(operand.shape, operand.dtype) for operand in operands),
             pltpu.VMEM((2, NK, 8, 2 * INNER), F32),
             pltpu.VMEM((HALF_K + 1, FRAMES, 2 * INNER), B16),
             pltpu.VMEM((HALF_K + 1, FRAMES, 2 * INNER), B16),
             pltpu.VMEM((NF, OWN, FRAMES), B16),
-            pltpu.VMEM((ITERS, NC * NQ, WROWS, 128), B16),
-            pltpu.VMEM((NX, COMP, 128), F32),
+            pltpu.VMEM((ITERS, NC * NS, COMP, 128), B16),
             pltpu.VMEM((COMP, 128), F32),
             pltpu.VMEM((COMP, FRAMES), F32),
             pltpu.VMEM((ITERS, NQ, ROWS, 128), F32),
             pltpu.VMEM((ITERS, NQ, ROWS, 128), F32),
-            pltpu.VMEM((ITERS, NQ, ROWS, 128), F32),
-            pltpu.VMEM((ITERS, NQ, ROWS, 128), F32),
-            pltpu.VMEM((ITERS, NZ, 4, 128), F32),
-            pltpu.VMEM((ITERS, NZ, 4, 128), F32),
-            pltpu.VMEM((ITERS, NZ, 4, 128), F32),
-            pltpu.VMEM((COMP, 128), F32),
-            pltpu.VMEM((8, 128), F32),
-            pltpu.VMEM((NX, COMP, 128), F32),
+            pltpu.VMEM((ITERS, NS, PACKED, 128), F32),
+            pltpu.VMEM((ITERS, NS, PACKED, 128), F32),
+            pltpu.VMEM((ITERS, NZ // 2, PACKED, 128), F32),
+            pltpu.VMEM((2 * NX, COMP, 128), F32),
             dma((GROUPS,)),
+            dma((8,)),
             dma((2,)),
             dma((ITERS, NY, 2)),
-            dma((ITERS, 2)),
             dma((ITERS, 2)),
             dma((ITERS, 2)),
             dma((2,)),
@@ -446,9 +482,9 @@
             dma((2,)),
         ],
         compiler_params=pltpu.CompilerParams(
-            collective_id=0, has_side_effects=True, vmem_limit_bytes=50 * 2**20
+            collective_id=0, has_side_effects=True, vmem_limit_bytes=64 * 2**20 - 2**16
         ),
-    )(audio, w_start, h_start, *constants)
+    )(*operands)
 
 
 def solution(mesh):

time: 89.7 us -> 77.5 us (0.86)
  local copies, waits for them, and re-layouts: 9.03 us -> 3.04 us
  Pallas kernels: 78.7 us -> 72.9 us
    unnamed x18 -> x2, local copies, waits for them, and re-layouts: 9.03 us -> 3.04 us
    pallas_call x1, Pallas kernels: 78.7 us -> 72.9 us  [shards(): pl.pallas_call(kernel, out_shape=(jax.ShapeDtypeStruct((COMP, OWN), F32),...]
where the time goes in v2:
time: 77.5 us; the launch traced here: 76.6 us
  Pallas kernels  72.9 us (94%)
  local copies, waits for them, and re-layouts  3.04 us (4%)
    pallas_call x1, Pallas kernels, shards(): pl.pallas_call(kernel, out_shape=(jax.ShapeDtypeStruct((COMP, OWN), F32),...  72.9 us
    unnamed x2, local copies, waits for them, and re-layouts  3.04 us

profile of v2, /device:TPU:6, one launch (start us, length us, event | category | flops | bytes accessed | tf_op | source)
XLA Modules:
  0.0 76.6 jit_solution(3290736557593748627)
XLA Ops:
  0.6 72.9 %shard_map.104 = (f32[32,512]{1,0:T(8,128)}, f32[32,1024]{1,0:T(8,128)}) custom-call(bf16[1,1048576]{1,0:T(2,128)(2,1)} %audio_hbm.1, f32[32,512]{1,0:T(8,128)} %w_hbm.1, f32[32,1024]{1,0:T(8,128)} %h_hbm.1, bf16[544,512]{1,0:T(8,128)(2,1)} %constant.12.clone.first_hi_hbm, bf16[544,512]{1,0:T(8,128)(2,1)} %constant.13.clone.first_lo_hbm, ...), custom_call_target="tpu_custom_call" | custom-call | tf_op jit(solution)/shard_map/pallas_call | solution.py:450
  73.5 1.5 %copy.13 = f32[32,512]{1,0:T(8,128)} copy(f32[32,512]{1,0:T(8,128)} %get-tuple-element.4) | data formatting | bytes 131072
  75.0 1.6 %copy.14 = f32[32,1024]{1,0:T(8,128)} copy(f32[32,1024]{1,0:T(8,128)} %get-tuple-element.5) | data formatting | bytes 262144

commit v3 on v2

--- a/solution.py
+++ b/solution.py
@@ -30,8 +30,9 @@
 GROUPS = FRAMES // GROUP
 HALF_K = OUTER // 2
 NK = HALF_K + 2
-ROWS = COMP + 8
-PACKED = COMP // 2 + 8
+PACKED = COMP // 2
+EARLY = 4
+START = NX * COMP + 16
 NS = 2 * NQ
 HALF = 64
 
@@ -110,6 +111,7 @@
     left = audio[:, pl.ds(start, span)].reshape(8 * OUTER, INNER)
     right = audio[:, pl.ds(start + span, span)].reshape(8 * OUTER, INNER)
     both = jnp.concatenate([left, right], axis=1)
+    outer = outer.at[lax.rem(g, 2)]
     outer[...] = (dot(first_hi[...], both) + dot(first_lo[...], both)).reshape(outer.shape)
     frame = pl.multiple_of(g * GROUP, GROUP)
 
@@ -136,7 +138,7 @@
 
     zero_re, zero_im = turned(0)
     one_re, one_im = turned(1)
-    lax.fori_loop(0, HALF_K + 1, step, (one_re, -one_im, zero_re, zero_im), unroll=3)
+    lax.fori_loop(0, HALF_K + 1, step, (one_re, -one_im, zero_re, zero_im), unroll=True)
 
 
 def second_stage(second_hi, second_lo, g_hi, g_lo, mag):
@@ -169,7 +171,7 @@
         put(HALF_K + 2 * p, out[64:, :FRAMES], out[64:, FRAMES:])
         return 0
 
-    lax.fori_loop(1, HALF_K // 2, step, 0)
+    lax.fori_loop(1, HALF_K // 2, step, 0, unroll=True)
 
 
 def kernel(
@@ -178,9 +180,11 @@
     w_out, h_out,
     audio, w_in, h_in, first_hi, first_lo, twist, second_hi, second_lo, place,
     outer, g_hi, g_lo, mag,
-    gathered, comp, act,
+    start, gathered, comp, act,
     send_core, recv_core, send_plane, recv_plane, sums, last,
+    gram_mine, gram_core, gram_z, gram_plane,
     audio_sem, load_sem, gather_sem, core_sems, plane_sem, z_sem, wide_sem, fwd_sem, last_sem, act_sem,
+    gram_core_sem, gram_z_sem, gram_plane_sem,
 ):
     f, t = lax.axis_index("freq"), lax.axis_index("tm")
     y, c = lax.div(f, NC), lax.rem(f, NC)
@@ -215,6 +219,12 @@
 
     def far_peer(i):
         return f, NX * (2 * lax.rem(far + i, NZ // 2) + m) + x
+
+    def z_peer(i):
+        return f, NX * lax.rem(z + i, NZ) + x
+
+    def plane_peer(i):
+        return slot_device(2 * lax.rem(q + i, NQ) + m)
 
     def load_audio(g):
         part = pl.ds(pl.multiple_of(g * span, span), span)
@@ -250,6 +260,7 @@
     for copy in loads[:3]:
         copy.start()
     each(1, NZ // 2, lambda i: signal(*far_peer(i)))
+    each(1, NZ // 2, lambda i: signal(f, NX * (2 * lax.rem(far + i, NZ // 2) + 1 - m) + x))
     each(1, NS, lambda i: signal(*near_peer(i)))
     each(0, NY, lambda i: signal(NC * i + (1 - c), t))
     each(1, GROUPS, lambda g: load_audio(g).start())
@@ -258,11 +269,13 @@
     for copy in loads[:3]:
         copy.wait()
 
-    def spectra(g):
-        load_audio(g).wait()
-        first_stage(audio, first_hi, first_lo, twist, outer, g_hi, g_lo, g)
-
-    each(0, GROUPS, spectra)
+    def spectra(p):
+        for g in (2 * p, 2 * p + 1):
+            load_audio(g).wait()
+        for g in (2 * p, 2 * p + 1):
+            first_stage(audio, first_hi, first_lo, twist, outer, g_hi, g_lo, g)
+
+    each(0, EARLY // 2, spectra)
 
     for copy in loads[3:]:
         copy.wait()
@@ -272,57 +285,71 @@
     spread = dot(jnp.concatenate(terms(w_in[...]), axis=0), place[...])
     spread = spread[:COMP] + spread[COMP : 2 * COMP] + spread[2 * COMP :]
     gram = dot_t(spread, spread, HIGHEST)
-    none = jnp.zeros_like(gram)
-    first_slot = c * NS + 2 * NX * y
+    gram = pack(gram)
+    hi = gram.astype(B16).astype(F32)
+    start[f, NX * COMP :, :] = jnp.concatenate([hi, gram - hi], axis=0).astype(B16)
     for j in range(NX):
         block = spread[:, 128 * j : 128 * j + 128]
         last[2 * j] = block
-        gathered[0, first_slot + 2 * j] = gather_slot(low, block, gram if j == 0 else none)
-        gathered[0, first_slot + 2 * j + 1] = gather_slot(lane >= HALF, block, none)
+        start[f, COMP * j : COMP * j + COMP, :] = block.astype(B16)
     comp[...] = last[2 * x]
     act[...] = h_in[:, pl.ds(pl.multiple_of(f * FRAMES, FRAMES), FRAMES)]
 
-    pl.semaphore_wait(pltpu.get_barrier_semaphore(), (NS - 1) + (NZ // 2 - 1) + NY)
+    pl.semaphore_wait(pltpu.get_barrier_semaphore(), (NS - 1) + 2 * (NZ // 2 - 1) + NY)
 
     def send_start(i):
-        slots = gathered.at[0, pl.ds(first_slot, 2 * NX)]
-        remote(slots, slots, gather_sem, lax.rem(f + i, NF), t).start()
+        remote(start.at[f], start.at[f], gather_sem, lax.rem(f + i, NF), t).start()
 
     each(1, NF, send_start)
+    each(EARLY // 2, GROUPS // 2, spectra)
     second_stage(second_hi, second_lo, g_hi, g_lo, mag)
-    drain(gathered.at[0, pl.ds(0, (NF - 1) * 2 * NX)], gather_sem.at[1])
+    drain(start.at[pl.ds(0, NF - 1)], gather_sem.at[1])
 
     for it in range(ITERS):
         def product(core):
             total = jnp.zeros((COMP, FRAMES), F32)
             for yy in range(NY):
-                first = core * NS + 2 * NX * yy
-                rows = [
-                    jnp.where(low, gathered[it, first + 2 * j], gathered[it, first + 2 * j + 1])
-                    for j in range(NX)
-                ]
+                if it == 0:
+                    rows = [start[NC * yy + core, COMP * j : COMP * j + COMP, :] for j in range(NX)]
+                else:
+                    first = core * NS + 2 * NX * yy
+                    rows = [
+                        jnp.where(low, gathered[first + 2 * j], gathered[first + 2 * j + 1])
+                        for j in range(NX)
+                    ]
                 total += dot(jnp.concatenate(rows, axis=1), mag[NC * yy + core])
             return total
 
         def gram_of(core):
+            total = jnp.zeros((COMP, 128), F32)
+
             def add(i, total):
                 at = core * NS + 2 * i
-                return total + jnp.where(low, gathered[it, at + 1], gathered[it, at]).astype(F32)
-
-            return lax.fori_loop(0, NQ, add, jnp.zeros((COMP, 128), F32), unroll=4)
+                return total + jnp.where(low, gathered[at + 1], gathered[at]).astype(F32)
+
+            return lax.fori_loop(0, NQ, add, total, unroll=4)
 
         numer_h = product(c)
-        gram_w = gram_of(c)
+        gram_w = gram_of(c) if it > 0 else None
         if it == 1:
-            drain(gathered.at[1, pl.ds(0, NS)], fwd_sem.at[1])
+            drain(gathered.at[pl.ds(0, NS)], fwd_sem.at[1])
         numer_h += product(1 - c)
-        gram_w += gram_of(1 - c)
-        gram_w = (gram_w[:, :32] + gram_w[:, 64:96]) + (gram_w[:, 32:64] + gram_w[:, 96:])
+        if it == 0:
+            total = start[0, NX * COMP :, :].astype(F32)
+            for i in range(1, NF):
+                total += start[i, NX * COMP :, :].astype(F32)
+            gram_w = unpack(total[:8] + total[8:])
+        else:
+            gram_w += gram_of(1 - c)
+            gram_w = (gram_w[:, :32] + gram_w[:, 64:96]) + (gram_w[:, 32:64] + gram_w[:, 96:])
         state = act[...]
         state = state * numer_h / dot(gram_w, state, HIGHEST)
         act[...] = state
         rounded = state.astype(B16)
-        gram_h = pack(dot_t(state, state, HIGHEST))
+        gram_mine[it] = pack(dot_t(state, state, HIGHEST))
+        remote(
+            gram_mine.at[it], gram_core.at[it], gram_core_sem.at[it], NC * y + (1 - c), t
+        ).start()
 
         core_sem = core_sems.at[it]
         order = (2, 1, 3, 0)
@@ -334,8 +361,7 @@
             yy = lax.rem(y + dy, NY)
             value = partial(NC * yy + (1 - c))
             for j in range(NX):
-                tile = jnp.concatenate([value[:, 128 * j : 128 * j + 128], gram_h], axis=0)
-                send_core[it, yy * NX + j] = tile
+                send_core[it, yy * NX + j] = value[:, 128 * j : 128 * j + 128]
             slots = pl.ds(yy * NX, NX)
             remote(
                 send_core.at[it, slots], recv_core.at[it, slots], core_sem.at[step],
@@ -347,13 +373,10 @@
             drain(recv_core.at[it, pl.ds(yy * NX, NX)], core_sem.at[step, 1])
             for j in range(NX):
                 chip = yy * NX + j
-                tile = jnp.concatenate([value[:, 128 * j : 128 * j + 128], gram_h], axis=0)
-                tile += recv_core[it, chip]
-                top, bottom, sum_h = tile[:16], tile[16:32], tile[32:]
-                left = jnp.where(low[:16], top, swap(bottom))
-                right = jnp.where(low[:16], swap(top), bottom)
-                send_plane[it, 2 * chip] = jnp.concatenate([left, sum_h], axis=0)
-                send_plane[it, 2 * chip + 1] = jnp.concatenate([right, sum_h], axis=0)
+                tile = value[:, 128 * j : 128 * j + 128] + recv_core[it, chip]
+                top, bottom = tile[:PACKED], tile[PACKED:]
+                send_plane[it, 2 * chip] = jnp.where(low[:PACKED], top, swap(bottom))
+                send_plane[it, 2 * chip + 1] = jnp.where(low[:PACKED], swap(top), bottom)
             for dx in range(NX):
                 xx = lax.rem(x + dx, NX)
                 for dm in range(2):
@@ -366,14 +389,14 @@
                             plane_sem.at[it], *slot_device(slot),
                         ).start()
 
-        if it == ITERS - 1:
-            columns = pl.ds(pl.multiple_of(f * FRAMES, FRAMES), FRAMES)
-            h_out[:, columns] = state
-
-            def send_act(i):
-                remote(act, h_out.at[:, columns], act_sem, lax.rem(f + i, NF), t).start()
-
-            each(1, NF, send_act)
+        drain(gram_core.at[it], gram_core_sem.at[it, 1])
+        gram_z[it, z] = gram_mine[it] + gram_core[it]
+
+        def gram_to_z(i):
+            own = gram_z.at[it, z]
+            remote(own, own, gram_z_sem.at[it], *z_peer(i)).start()
+
+        each(1, NZ, gram_to_z)
 
         drain(recv_plane.at[it, pl.ds(0, NS - 1)], plane_sem.at[it, 1])
         total = recv_plane[it, 0]
@@ -386,31 +409,55 @@
             remote(own, own, z_sem.at[it], *far_peer(i)).start()
 
         each(1, NZ // 2, share)
+        drain(gram_z.at[it, pl.ds(0, NZ - 1)], gram_z_sem.at[it, 1])
+        gram_h = gram_z[it, 0]
+        for i in range(1, NZ):
+            gram_h += gram_z[it, i]
+        gram_plane[it, q] = gram_h
+
+        def gram_to_plane(i):
+            own = gram_plane.at[it, q]
+            remote(own, own, gram_plane_sem.at[it], *plane_peer(i)).start()
+
+        each(1, NQ, gram_to_plane)
+        if it == ITERS - 1:
+            columns = pl.ds(pl.multiple_of(f * FRAMES, FRAMES), FRAMES)
+            h_out[:, columns] = state
+
+            def send_act(i):
+                remote(act, h_out.at[:, columns], act_sem, lax.rem(f + i, NF), t).start()
+
+            each(1, NF, send_act)
+
         drain(sums.at[it, pl.ds(0, NZ // 2 - 1)], z_sem.at[it, 1])
         total = sums[it, 0]
         for i in range(1, NZ // 2):
             total += sums[it, i]
-        packed = total[:16]
+        drain(gram_plane.at[it, pl.ds(0, NQ - 1)], gram_plane_sem.at[it, 1])
+        gram_h = gram_plane[it, 0]
+        for i in range(1, NQ):
+            gram_h += gram_plane[it, i]
+        packed = total
         other = swap(packed)
         numer_w = jnp.concatenate(
             [jnp.where(m == 0, packed, other), jnp.where(m == 0, other, packed)], axis=0
         )
         own = comp[...]
-        below = dot(unpack(total[16:]), own, HIGHEST)
+        below = dot(unpack(gram_h), own, HIGHEST)
         own = jnp.where(mine, own * numer_w / jnp.where(mine, below, 1.0), 0.0)
         comp[...] = own
 
         if it < ITERS - 1:
             at = c * NS + own_slot
-            gathered[it + 1, at] = gather_slot(mine, own, dot_t(own, own, HIGHEST))
+            gathered[at] = gather_slot(mine, own, dot_t(own, own, HIGHEST))
 
             def spread_near(i):
-                slot = gathered.at[it + 1, at]
+                slot = gathered.at[at]
                 remote(slot, slot, wide_sem, *near_peer(i)).start()
 
             each(1, NS, spread_near)
-            drain(gathered.at[it + 1, pl.ds(0, NS - 1)], wide_sem.at[1])
-            slots = gathered.at[it + 1, pl.ds(c * NS, NS)]
+            drain(gathered.at[pl.ds(0, NS - 1)], wide_sem.at[1])
+            slots = gathered.at[pl.ds(c * NS, NS)]
             remote(slots, slots, fwd_sem, NC * y + (1 - c), t).start()
         else:
             end = 2 * x + m
@@ -431,15 +478,18 @@
 
     drain(h_out.at[:, pl.ds(0, (NF - 1) * FRAMES)], act_sem.at[1])
     drain(h_out.at[:, pl.ds(0, (NF - 1) * FRAMES)], act_sem.at[0])
-    drain(gathered.at[0, pl.ds(0, (NF - 1) * 2 * NX)], gather_sem.at[0])
-    drain(gathered.at[1, pl.ds(0, NS - 1)], wide_sem.at[0])
-    drain(gathered.at[1, pl.ds(0, NS)], fwd_sem.at[0])
+    drain(start.at[pl.ds(0, NF - 1)], gather_sem.at[0])
+    drain(gathered.at[pl.ds(0, NS - 1)], wide_sem.at[0])
+    drain(gathered.at[pl.ds(0, NS)], fwd_sem.at[0])
     drain(last.at[pl.ds(0, 2 * NX - 1)], last_sem.at[0])
     for it in range(ITERS):
         for step in range(NY):
             drain(send_core.at[it, pl.ds(0, NX)], core_sems.at[it, step, 0])
         drain(send_plane.at[it, pl.ds(0, NS - 1)], plane_sem.at[it, 0])
         drain(sums.at[it, pl.ds(0, NZ // 2 - 1)], z_sem.at[it, 0])
+        drain(gram_mine.at[it], gram_core_sem.at[it, 0])
+        drain(gram_z.at[it, pl.ds(0, NZ - 1)], gram_z_sem.at[it, 0])
+        drain(gram_plane.at[it, pl.ds(0, NQ - 1)], gram_plane_sem.at[it, 0])
 
 
 def shards(audio, w_start, h_start):
@@ -457,19 +507,24 @@
         out_specs=(vmem, vmem),
         scratch_shapes=[
             *(pltpu.VMEM(operand.shape, operand.dtype) for operand in operands),
-            pltpu.VMEM((2, NK, 8, 2 * INNER), F32),
+            pltpu.VMEM((2, 2, NK, 8, 2 * INNER), F32),
             pltpu.VMEM((HALF_K + 1, FRAMES, 2 * INNER), B16),
             pltpu.VMEM((HALF_K + 1, FRAMES, 2 * INNER), B16),
             pltpu.VMEM((NF, OWN, FRAMES), B16),
-            pltpu.VMEM((ITERS, NC * NS, COMP, 128), B16),
+            pltpu.VMEM((NF, START, 128), B16),
+            pltpu.VMEM((NC * NS, COMP, 128), B16),
             pltpu.VMEM((COMP, 128), F32),
             pltpu.VMEM((COMP, FRAMES), F32),
-            pltpu.VMEM((ITERS, NQ, ROWS, 128), F32),
-            pltpu.VMEM((ITERS, NQ, ROWS, 128), F32),
+            pltpu.VMEM((ITERS, NQ, COMP, 128), F32),
+            pltpu.VMEM((ITERS, NQ, COMP, 128), F32),
             pltpu.VMEM((ITERS, NS, PACKED, 128), F32),
             pltpu.VMEM((ITERS, NS, PACKED, 128), F32),
             pltpu.VMEM((ITERS, NZ // 2, PACKED, 128), F32),
             pltpu.VMEM((2 * NX, COMP, 128), F32),
+            pltpu.VMEM((ITERS, 8, 128), F32),
+            pltpu.VMEM((ITERS, 8, 128), F32),
+            pltpu.VMEM((ITERS, NZ, 8, 128), F32),
+            pltpu.VMEM((ITERS, NQ, 8, 128), F32),
             dma((GROUPS,)),
             dma((8,)),
             dma((2,)),
@@ -480,6 +535,9 @@
             dma((2,)),
             dma((2,)),
             dma((2,)),
+            dma((ITERS, 2)),
+            dma((ITERS, 2)),
+            dma((ITERS, 2)),
         ],
         compiler_params=pltpu.CompilerParams(
             collective_id=0, has_side_effects=True, vmem_limit_bytes=64 * 2**20 - 2**16

time: 77.5 us -> 74.2 us (0.957)
  Pallas kernels: 72.9 us -> 70.3 us
    pallas_call x1, Pallas kernels: 72.9 us -> 70.3 us  [shards(): pl.pallas_call(kernel, out_shape=(jax.ShapeDtypeStruct((COMP, OWN), F32),...]
where the time goes in v3:
time: 74.2 us; the launch traced here: 74 us
  Pallas kernels  70.3 us (95%)
  local copies, waits for them, and re-layouts  3.04 us (4%)
    pallas_call x1, Pallas kernels, shards(): pl.pallas_call(kernel, out_shape=(jax.ShapeDtypeStruct((COMP, OWN), F32),...  70.3 us
    unnamed x2, local copies, waits for them, and re-layouts  3.04 us

profile of v3, /device:TPU:6, one launch (start us, length us, event | category | flops | bytes accessed | tf_op | source)
XLA Modules:
  0.0 74.0 jit_solution(10948087494712547162)
XLA Ops:
  0.6 70.3 %shard_map.104 = (f32[32,512]{1,0:T(8,128)}, f32[32,1024]{1,0:T(8,128)}) custom-call(bf16[1,1048576]{1,0:T(2,128)(2,1)} %audio_hbm.1, f32[32,512]{1,0:T(8,128)} %w_hbm.1, f32[32,1024]{1,0:T(8,128)} %h_hbm.1, bf16[544,512]{1,0:T(8,128)(2,1)} %constant.12.clone.first_hi_hbm, bf16[544,512]{1,0:T(8,128)(2,1)} %constant.13.clone.first_lo_hbm, ...), custom_call_target="tpu_custom_call" | custom-call | tf_op jit(solution)/shard_map/pallas_call | solution.py:500
  70.9 1.5 %copy.13 = f32[32,512]{1,0:T(8,128)} copy(f32[32,512]{1,0:T(8,128)} %get-tuple-element.4) | data formatting | bytes 131072
  72.4 1.6 %copy.14 = f32[32,1024]{1,0:T(8,128)} copy(f32[32,1024]{1,0:T(8,128)} %get-tuple-element.5) | data formatting | bytes 262144

commit v4 on v3

--- a/solution.py
+++ b/solution.py
@@ -492,18 +492,38 @@
         drain(gram_plane.at[it, pl.ds(0, NQ - 1)], gram_plane_sem.at[it, 0])
 
 
+def deliver(w_ref, h_ref, w_out, h_out, w_held, h_held, sem):
+    into = (
+        pltpu.make_async_copy(w_ref, w_held, sem.at[0]),
+        pltpu.make_async_copy(h_ref, h_held, sem.at[1]),
+    )
+    out = (
+        pltpu.make_async_copy(w_held, w_out, sem.at[2]),
+        pltpu.make_async_copy(h_held, h_out, sem.at[3]),
+    )
+    for copy in into:
+        copy.start()
+    for load, store in zip(into, out):
+        load.wait()
+        store.start()
+    for store in out:
+        store.wait()
+
+
 def shards(audio, w_start, h_start):
     vmem = pl.BlockSpec(memory_space=pltpu.VMEM)
     dma = pltpu.SemaphoreType.DMA
     constants = [jnp.asarray(table) for table in tables()]
     operands = (audio, w_start, h_start, *constants)
-    return pl.pallas_call(
+    hbm = pl.BlockSpec(memory_space=pltpu.HBM)
+    shapes = (
+        jax.ShapeDtypeStruct((COMP, OWN), F32),
+        jax.ShapeDtypeStruct((COMP, NF * FRAMES), F32),
+    )
+    results = pl.pallas_call(
         kernel,
-        out_shape=(
-            jax.ShapeDtypeStruct((COMP, OWN), F32),
-            jax.ShapeDtypeStruct((COMP, NF * FRAMES), F32),
-        ),
-        in_specs=[pl.BlockSpec(memory_space=pltpu.HBM)] * len(operands),
+        out_shape=shapes,
+        in_specs=[hbm] * len(operands),
         out_specs=(vmem, vmem),
         scratch_shapes=[
             *(pltpu.VMEM(operand.shape, operand.dtype) for operand in operands),
@@ -543,6 +563,14 @@
             collective_id=0, has_side_effects=True, vmem_limit_bytes=64 * 2**20 - 2**16
         ),
     )(*operands)
+    return pl.pallas_call(
+        deliver,
+        out_shape=shapes,
+        in_specs=[hbm] * 2,
+        out_specs=(hbm, hbm),
+        scratch_shapes=[*(pltpu.VMEM(shape.shape, F32) for shape in shapes), dma((4,))],
+        compiler_params=pltpu.CompilerParams(vmem_limit_bytes=64 * 2**20 - 2**16),
+    )(*results)
 
 
 def solution(mesh):

time: 74.2 us -> 72.7 us (0.980)
  local copies, waits for them, and re-layouts: 3.04 us -> 0 us
  Pallas kernels: 70.3 us -> 71.9 us
    unnamed x2 -> x0, local copies, waits for them, and re-layouts: 3.04 us -> none
    pallas_call x1 -> x2, Pallas kernels: 70.3 us -> 71.9 us  [the longest x1 70.3 us: shards(): pl.pallas_call(kernel, out_shape=shapes, in_specs=[hbm] * len(operands),...]
where the time goes in v4:
time: 72.7 us; the launch traced here: 72.5 us
  Pallas kernels  71.9 us (99%)
    pallas_call x1, Pallas kernels, shards(): pl.pallas_call(kernel, out_shape=shapes, in_specs=[hbm] * len(operands),...  70.3 us
    pallas_call x1, Pallas kernels, shards(): pl.pallas_call(deliver, out_shape=shapes, in_specs=[hbm] * 2, out_specs=(...  1.63 us

profile of v4, /device:TPU:6, one launch (start us, length us, event | category | flops | bytes accessed | tf_op | source)
XLA Modules:
  0.0 72.5 jit_solution(5747767566026540692)
XLA Ops:
  0.6 70.3 %shard_map.104 = (f32[32,512]{1,0:T(8,128)}, f32[32,1024]{1,0:T(8,128)}) custom-call(bf16[1,1048576]{1,0:T(2,128)(2,1)} %audio_hbm.1, f32[32,512]{1,0:T(8,128)} %w_hbm.1, f32[32,1024]{1,0:T(8,128)} %h_hbm.1, bf16[544,512]{1,0:T(8,128)(2,1)} %constant.12.clone.first_hi_hbm, bf16[544,512]{1,0:T(8,128)(2,1)} %constant.13.clone.first_lo_hbm, ...), custom_call_target="tpu_custom_call" | custom-call | tf_op jit(solution)/shard_map/pallas_call | solution.py:523
  70.9 1.6 %shard_map.105 = (f32[32,512]{1,0:T(8,128)}, f32[32,1024]{1,0:T(8,128)}) custom-call(f32[32,512]{1,0:T(8,128)} %get-tuple-element.4.w_ref, f32[32,1024]{1,0:T(8,128)} %get-tuple-element.5.h_ref), custom_call_target="tpu_custom_call" | custom-call | tf_op jit(solution)/shard_map/pallas_call | solution.py:566
